TPU v7x, 32 devices: a whole 2x2x4 slice. The times are simulated.
32 devices in a mesh: prow: 8 (over z, x), pcol: 4 (over y, core).
Axes of the slice: x: 2, y: 2, z: 4, core: 2. Of those that a mesh axis runs over, the one named last changes fastest.
Arguments:
- sigma_top: bfloat16 [8192, 8192], P('prow', 'pcol'), may hold values from -400 to 400, as said below
- panel_par: bfloat16 [8192, 1024], P('prow', 'pcol'), may hold values from -0.119628906 to 0.119628906
- panel_kid: bfloat16 [8192, 2048], P('prow', 'pcol'), may hold values from -0.119628906 to 0.119628906
- link_kid: bfloat16 [8, 256, 256], P('pcol'), may hold values from -0.23925781 to 0.23925781
- dinv_par: float32 [4, 256, 256], P('pcol'), may hold values from -6 to 6
- dinv_kid: float32 [8, 256, 256], P('pcol'), may hold values from -6 to 6
- mask_par: int32 [4, 32], P('pcol', 'prow'), may hold values 0 or 1
- mask_kid: int32 [8, 32], P('pcol', 'prow'), may hold values 0 or 1
Outputs:
- sigma_par: bfloat16 [8192, 1024], P('prow', 'pcol')
- diag_par: float32 [4, 256, 256], P('pcol')
- sigma_kid: bfloat16 [8192, 2048], P('prow', 'pcol')
- link_sigma: float32 [8, 256, 256], P('pcol')
- diag_kid: float32 [8, 256, 256], P('pcol')
Inputs may be any that keep to these rules, and one draw needn't show every extreme that they name: `sigma_top`: symmetric.
All inputs are finite; a program needn't handle non-finite values. No bound on the sum of `mask_par` or of `mask_kid` on one device may be relied on, other than what follows from the above.
Results may differ from a plain program's by a relative error of at most 0.015.
Values may be sent and summed in bfloat16 or wider, within the bound.
A program may use at most 64 MiB of HBM per device.

v0:
```python
import jax
import jax.numpy as jnp
from jax import lax
from jax.sharding import PartitionSpec as P

KIDS = 2


def expand_rows(mask, width):
    count, blocks = mask.shape
    spread = jnp.broadcast_to(
        mask.T.astype(jnp.float32)[:, None, :, None], (blocks, width, count, width)
    )
    return spread.reshape(blocks * width, count * width)


def batch_mult(left, right):
    return jnp.einsum("cab,cbd->cad", left, right, precision=lax.Precision.HIGHEST)


def batch_tmult(left, right):
    return jnp.einsum("cba,cbd->cad", left, right, precision=lax.Precision.HIGHEST)


def on_device(sigma_top, panel_par, panel_kid, link_kid, dinv_par, dinv_kid, mask_par, mask_kid):
    width = dinv_par.shape[1]
    par_here = dinv_par.shape[0]
    kid_here = dinv_kid.shape[0]
    row_count = sigma_top.shape[0]
    kid_pattern = mask_kid * jnp.repeat(mask_par, KIDS, axis=0)
    par_rows = expand_rows(mask_par, width)
    kid_rows = expand_rows(kid_pattern, width)
    low_par = panel_par * par_rows.astype(jnp.bfloat16)
    low_kid = panel_kid * kid_rows.astype(jnp.bfloat16)
    sigma_rows = lax.all_gather(sigma_top, "pcol", axis=1, tiled=True)
    prod_par = jnp.dot(
        sigma_rows,
        lax.all_gather(low_par, "prow", axis=0, tiled=True),
        preferred_element_type=jnp.float32,
    )
    prod_kid = jnp.dot(
        sigma_rows,
        lax.all_gather(low_kid, "prow", axis=0, tiled=True),
        preferred_element_type=jnp.float32,
    )
    sigma_par = (-prod_par * par_rows).astype(jnp.bfloat16)
    par_blocks = sigma_par.reshape(row_count, par_here, width)
    par_spread = jnp.repeat(par_blocks, KIDS, axis=1)
    carried = jnp.einsum("rcb,cbd->rcd", par_spread, link_kid, preferred_element_type=jnp.float32)
    sigma_kid = (-(prod_kid + carried.reshape(row_count, kid_here * width)) * kid_rows).astype(
        jnp.bfloat16
    )
    low_par3 = low_par.reshape(row_count, par_here, width)
    low_kid3 = low_kid.reshape(row_count, kid_here, width)
    kid_blocks = sigma_kid.reshape(row_count, kid_here, width)
    part_par = jnp.einsum("rpb,rpd->pbd", low_par3, par_blocks, preferred_element_type=jnp.float32)
    part_cross = jnp.einsum(
        "rcb,rcd->cbd", par_spread, low_kid3, preferred_element_type=jnp.float32
    )
    part_kid = jnp.einsum("rcb,rcd->cbd", low_kid3, kid_blocks, preferred_element_type=jnp.float32)
    link_wide = link_kid.astype(jnp.float32)
    sum_par = lax.psum(part_par.astype(jnp.bfloat16), "prow").astype(jnp.float32)
    diag_par = dinv_par - sum_par
    diag_spread = jnp.repeat(diag_par, KIDS, axis=0)
    cross_sum, kid_sum = (
        lax.psum(part_cross.astype(jnp.bfloat16), "prow").astype(jnp.float32),
        lax.psum(part_kid.astype(jnp.bfloat16), "prow").astype(jnp.float32),
    )
    link_sigma = -(cross_sum + batch_mult(diag_spread, link_wide))
    diag_kid = dinv_kid - kid_sum - batch_tmult(link_wide, link_sigma)
    return (sigma_par, diag_par, sigma_kid, link_sigma, diag_kid)


def solution(mesh):
    placed = (
        P("prow", "pcol"),
        P("prow", "pcol"),
        P("prow", "pcol"),
        P("pcol", None, None),
        P("pcol", None, None),
        P("pcol", None, None),
        P("pcol", "prow"),
        P("pcol", "prow"),
    )
    return jax.shard_map(
        on_device,
        mesh=mesh,
        in_specs=placed,
        out_specs=(
            P("prow", "pcol"),
            P("pcol", None, None),
            P("prow", "pcol"),
            P("pcol", None, None),
            P("pcol", None, None),
        ),
        check_vma=False,
    )
```

profile of v0, /device:TPU:0, one launch (start us, length us, event | category | flops | bytes accessed | tf_op | source)
XLA Modules:
  0.0 421.5 jit_solution(7698292222596817835)
XLA Ops:
  7.2 0.0 copy-start
  7.2 0.0 copy-start.11
  7.2 0.0 copy-start.6
  7.2 0.0 copy-start.10
  7.2 0.0 all-gather.4.cloned.1.call-start
  7.3 0.7 bitcast_convert_fusion
  8.0 0.1 broadcast_bitcast_fusion
  8.1 2.0 broadcast_multiply_fusion
  10.1 0.0 all-gather.4.cloned.1.call-update
  10.2 0.0 all-gather.6.cloned.1.call-start
  10.2 0.7 all-gather.6.cloned.1.call-update
  10.9 0.0 all-gather.8.cloned.1.call-start
  11.0 0.0 copy-done.6
  11.0 1.3 copy.13
  12.3 0.0 copy-done.11
  12.3 0.0 copy-done.10
  12.3 0.3 broadcast_in_dim.25
  12.6 0.5 copy.29
  13.1 0.4 copy-done.3
  13.5 1.2 convert_multiply_fusion
  14.7 0.0 all-gather.8.cloned.1.call-update
  14.7 0.0 copy-start.1
  14.8 0.0 all-reduce.3.cloned.1.call-start
  14.8 72.1 %all-gather.4.cloned.1.call-done = bf16[8192,256]{1,0:T(8,128)(2,1)} async-done(((bf16[1024,256]{1,0:T(8,128)(2,1)}), bf16[8192,256]{1,0:T(8,128)(2,1)}) %all-gather.4.cloned.1.call-update) | async-done | bytes 4194320 | tf_op jit(solution)/shard_map/all_gather | solution.py:38
  86.9 105.8 %all-gather.6.cloned.1.call-done = bf16[1024,8192]{1,0:T(8,128)(2,1)} async-done(((bf16[1024,2048]{1,0:T(8,128)(2,1)}), bf16[1024,8192]{1,0:T(8,128)(2,1)}) %all-gather.6.cloned.1.call-update) | async-done | bytes 16777232 | tf_op jit(solution)/shard_map/all_gather | solution.py:35
  192.7 11.6 %fusion.4 = bf16[256,1024]{1,0:T(8,128)(2,1)S(1)} fusion(bf16[8192,256]{1,0:T(8,128)(2,1)} %all-gather.4.cloned.1.call-done, bf16[1024,8192]{1,0:T(8,128)(2,1)} %all-gather.6.cloned.1.call-done, f32[1024]{0:T(1024)S(1)} %bitcast.58), kind=kOutput, calls=%fused_computation.6 | convolution fusion | flops 4295753728 | bytes 21499904 | tf_op jit(solution)/shard_map/dot_general | solution.py:36
  204.3 0.0 copy-done.1
  204.3 1.0 fusion.7
  205.3 2.4 convolution_convert_fusion.1
  207.7 0.0 copy-done
  207.7 1.9 fusion.9
  209.6 110.7 %all-gather.8.cloned.1.call-done = bf16[8192,512]{0,1:T(8,128)(2,1)} async-done(((bf16[1024,512]{0,1:T(8,128)(2,1)}), bf16[8192,512]{0,1:T(8,128)(2,1)}) %all-gather.8.cloned.1.call-update) | async-done | bytes 8388624 | tf_op jit(solution)/shard_map/all_gather | solution.py:43
  320.4 15.2 %fusion.2 = bf16[1024,512]{0,1:T(8,128)(2,1)S(1)} fusion(f32[1024,512]{0,1:T(8,128)S(1)} %bitcast.48, f32[2,1024,256]{1,2,0:T(8,128)} %fusion.9, bf16[8192,512]{0,1:T(8,128)(2,1)} %all-gather.8.cloned.1.call-done, bf16[1024,8192]{1,0:T(8,128)(2,1)} %all-gather.6.cloned.1.call-done), kind=kOutput, calls=%fused_computation.3 | convolution fusion | flops 8592031744 | bytes 30408704 | tf_op jit(solution)/shard_map/dot_general | solution.py:41
  335.6 0.0 copy-start.9
  335.6 0.0 copy-start.8
  335.7 1.0 copy-done.7
  336.6 1.2 convolution_convert_fusion
  337.8 0.0 all-reduce.3.cloned.1.call-update
  337.8 1.0 copy.20
  338.8 2.3 copy.21
  341.1 69.0 %all-reduce.3.cloned.1.call-done = (bf16[1,256,256]{2,1,0:T(8,128)(2,1)}, bf16[2,256,256]{2,1,0:T(8,128)(2,1)}, bf16[2,256,256]{2,1,0:T(8,128)(2,1)}) async-done(((bf16[1,256,256]{2,1,0:T(8,128)(2,1)}, bf16[2,256,256]{2,1,0:T(8,128)(2,1)}, bf16[2,256,256]{2,1,0:T(8,128)(2,1)}), (bf16[1,256,256]{2,1,0:T(8,128)(2,1)}, bf16[2,256,256]{2,1,0:T(8,128)(2,1)}, ...) | async-done | bytes 655376 | tf_op jit(solution)/shard_map/psum | solution.py:62
  410.1 0.0 copy-done.9
  410.1 0.9 convert_subtract_fusion
  411.1 0.0 copy-start.5
  411.1 1.5 fusion.6
  412.5 0.0 copy-start.4
  412.6 0.0 copy-done.8
  412.6 2.4 fusion.5
  (9 shorter events, 0.0 us)
Async XLA Ops:
  7.2 200.6 %copy-start = (bf16[2,256,256]{2,1,0:T(8,128)(2,1)S(1)}, bf16[2,256,256]{2,1,0:T(8,128)(2,1)}, u32[]{:S(2)}) copy-start(bf16[2,256,256]{2,1,0:T(8,128)(2,1)} %param.11) | copy-start | bytes 786436
  7.2 5.1 %copy-start.11 = (s32[1,4]{1,0:T(1,128)S(1)}, s32[1,4]{1,0:T(1,128)}, u32[]{:S(2)}) copy-start(s32[1,4]{1,0:T(1,128)} %param.14) | copy-start | bytes 52
  7.2 3.8 copy-start.6
  7.2 5.1 %copy-start.10 = (s32[2,4]{1,0:T(2,128)S(1)}, s32[2,4]{1,0:T(2,128)}, u32[]{:S(2)}) copy-start(s32[2,4]{1,0:T(2,128)} %param.15) | copy-start | bytes 100
  7.2 79.7 %all-gather.4.cloned.1.call-start = ((), (), s32[]{:S(2)}) async-start(), calls=%async_computation | async-start | bytes 4718592 | tf_op jit(solution)/shard_map/all_gather | solution.py:38
  10.2 182.5 %all-gather.6.cloned.1.call-start = ((), (), s32[]{:S(2)}) async-start(), calls=%async_computation.1 | async-start | bytes 20971520 | tf_op jit(solution)/shard_map/all_gather | solution.py:35
  10.9 309.5 %all-gather.8.cloned.1.call-start = ((), (), s32[]{:S(2)}) async-start(), calls=%async_computation.2 | async-start | bytes 9437184 | tf_op jit(solution)/shard_map/all_gather | solution.py:43
  12.3 1.2 copy-start.3
  14.7 189.5 %copy-start.1 = (bf16[1024,256]{1,0:T(8,128)(2,1)S(1)}, bf16[1024,256]{1,0:T(8,128)(2,1)}, u32[]{:S(2)}) copy-start(bf16[1024,256]{1,0:T(8,128)(2,1)} %broadcast_multiply_fusion) | copy-start | bytes 1572868
  14.8 395.4 %all-reduce.3.cloned.1.call-start = ((), (), s32[]{:S(2)}) async-start(), calls=%async_computation.3 | async-start | bytes 1310720 | tf_op jit(solution)/shard_map/psum | solution.py:62
  320.4 16.3 %copy-start.2 = (bf16[1024,512]{0,1:T(8,128)(2,1)S(1)}, bf16[1024,512]{0,1:T(8,128)(2,1)}, u32[]{:S(2)}) copy-start(bf16[1024,512]{0,1:T(8,128)(2,1)} %convert_multiply_fusion) | copy-start | bytes 3145732
  335.6 1.0 copy-start.7
  335.6 74.5 %copy-start.9 = (f32[1,256,256]{2,1,0:T(8,128)S(1)}, f32[1,256,256]{2,1,0:T(8,128)}, u32[]{:S(2)}) copy-start(f32[1,256,256]{2,1,0:T(8,128)} %param.12) | copy-start | bytes 786436
  335.6 76.9 %copy-start.8 = (f32[2,256,256]{2,1,0:T(8,128)S(1)}, f32[2,256,256]{2,1,0:T(8,128)}, u32[]{:S(2)}) copy-start(f32[2,256,256]{2,1,0:T(8,128)} %param.13) | copy-start | bytes 1572868
  411.1 3.9 copy-start.5
  412.5 2.4 copy-start.4
Sparse Core Ops, SparseCore 0:
  10.7 76.0 all-gather.3
  88.4 104.1 all-gather.5
  195.4 124.9 all-gather.7
  337.9 72.1 all-reduce.2
where the time goes:
time: 422 us
  waiting for transfers between devices  358 us (85%)
  matrix products  37.2 us (9%)
  between operations  13.9 us (3%)
  local copies, waits for them, and re-layouts  6.89 us (2%)
  other arithmetic  4.93 us (1%)
    all_gather x1, waiting for transfers between devices, on_device(): lax.all_gather(low_kid, 'prow', axis=0, tiled=True)  111 us
    all_gather x1, waiting for transfers between devices, on_device(): sigma_rows = lax.all_gather(sigma_top, 'pcol', axis=1, tiled=True)  106 us
    all_gather x1, waiting for transfers between devices, on_device(): lax.all_gather(low_par, 'prow', axis=0, tiled=True)  72.1 us
    psum x1, waiting for transfers between devices, on_device(): lax.psum(part_par.astype(jnp.bfloat16), 'prow').astype(jnp.float32)  69 us
    dot_general x1, matrix products, on_device(): jnp.dot(sigma_rows, lax.all_gather(low_kid, 'prow', axis=0, tiled=True),...  15.2 us
    dot_general x1, matrix products, on_device(): jnp.dot(sigma_rows, lax.all_gather(low_par, 'prow', axis=0, tiled=True),...  11.6 us
  transfers between devices with their start and end apart: 4, of which 4 were waited for; matrix products, arithmetic and copies ran while one was open for 6% of the time, Pallas kernels for 0%

commit v1 on v0

--- a/solution.py
+++ b/solution.py
@@ -59,7 +59,9 @@
     )
     part_kid = jnp.einsum("rcb,rcd->cbd", low_kid3, kid_blocks, preferred_element_type=jnp.float32)
     link_wide = link_kid.astype(jnp.float32)
-    sum_par = lax.psum(part_par.astype(jnp.bfloat16), "prow").astype(jnp.float32)
+    sum_par = jnp.sum(lax.all_gather(part_par.astype(jnp.bfloat16), "prow"), axis=0).astype(
+        jnp.float32
+    )
     diag_par = dinv_par - sum_par
     diag_spread = jnp.repeat(diag_par, KIDS, axis=0)
     cross_sum, kid_sum = (

time: 422 us -> 447 us (1.059)
  waiting for transfers between devices: 358 us -> 387 us
    all_gather x0 -> x1, waiting for transfers between devices: none -> 20 us  [on_device(): lax.all_gather(part_par.astype(jnp.bfloat16), 'prow')]
    psum x1, waiting for transfers between devices: 69 us -> 73.9 us  [on_device(): lax.psum(part_cross.astype(jnp.bfloat16), 'prow').astype(jnp.float32)]
  transfers between devices with their start and end apart: 4 -> 5, of which waited for: 4 -> 5; matrix products, arithmetic and copies ran while one was open for 6% -> 9% of each run, Pallas kernels for 0% -> 0%
where the time goes in v1:
time: 447 us
  waiting for transfers between devices  387 us (87%)
  matrix products  35.9 us (8%)
  between operations  14 us (3%)
  other arithmetic  5.3 us (1%)
  local copies, waits for them, and re-layouts  4.75 us (1%)
    all_gather x1, waiting for transfers between devices, on_device(): lax.all_gather(low_kid, 'prow', axis=0, tiled=True)  113 us
    all_gather x1, waiting for transfers between devices, on_device(): sigma_rows = lax.all_gather(sigma_top, 'pcol', axis=1, tiled=True)  106 us
    psum x1, waiting for transfers between devices, on_device(): lax.psum(part_cross.astype(jnp.bfloat16), 'prow').astype(jnp.float32)  73.9 us
    all_gather x1, waiting for transfers between devices, on_device(): lax.all_gather(low_par, 'prow', axis=0, tiled=True)  73.3 us
    all_gather x1, waiting for transfers between devices, on_device(): lax.all_gather(part_par.astype(jnp.bfloat16), 'prow')  20 us
    dot_general x1, matrix products, on_device(): jnp.dot(sigma_rows, lax.all_gather(low_kid, 'prow', axis=0, tiled=True),...  15.2 us
    dot_general x1, matrix products, on_device(): jnp.dot(sigma_rows, lax.all_gather(low_par, 'prow', axis=0, tiled=True),...  11.6 us
  transfers between devices with their start and end apart: 5, of which 5 were waited for; matrix products, arithmetic and copies ran while one was open for 9% of the time, Pallas kernels for 0%

profile of v1, /device:TPU:0, one launch (start us, length us, event | category | flops | bytes accessed | tf_op | source)
XLA Modules:
  0.0 447.0 jit_solution(16070720220527088607)
XLA Ops:
  7.2 0.0 copy-start
  7.2 0.0 copy-start.10
  7.2 0.0 copy-start.5
  7.2 0.0 copy-start.9
  7.2 0.0 all-gather.6.cloned.1.call-start
  7.3 0.7 bitcast_convert_fusion
  8.0 0.1 broadcast_bitcast_fusion
  8.1 2.0 broadcast_multiply_fusion
  10.1 0.0 all-gather.6.cloned.1.call-update
  10.2 0.0 all-gather.8.cloned.1.call-start
  10.2 0.7 all-gather.8.cloned.1.call-update
  10.9 0.0 all-gather.10.cloned.1.call-start
  11.0 0.0 copy-done.5
  11.0 0.5 copy.13
  11.5 0.0 copy-done.10
  11.5 0.0 copy-done.9
  11.5 0.3 broadcast_in_dim.25
  11.9 0.5 copy.29
  12.4 1.1 convert_multiply_fusion
  13.5 0.0 all-gather.10.cloned.1.call-update
  13.5 0.0 copy-start.1
  13.5 0.0 all-gather.12.cloned.1.call-start
  13.6 73.3 %all-gather.6.cloned.1.call-done = bf16[8192,256]{1,0:T(8,128)(2,1)} async-done(((bf16[1024,256]{1,0:T(8,128)(2,1)}), bf16[8192,256]{1,0:T(8,128)(2,1)}) %all-gather.6.cloned.1.call-update) | async-done | bytes 4194320 | tf_op jit(solution)/shard_map/all_gather | solution.py:38
  86.9 105.8 %all-gather.8.cloned.1.call-done = bf16[1024,8192]{1,0:T(8,128)(2,1)} async-done(((bf16[1024,2048]{1,0:T(8,128)(2,1)}), bf16[1024,8192]{1,0:T(8,128)(2,1)}) %all-gather.8.cloned.1.call-update) | async-done | bytes 16777232 | tf_op jit(solution)/shard_map/all_gather | solution.py:35
  192.7 11.6 %fusion.4 = bf16[256,1024]{1,0:T(8,128)(2,1)S(1)} fusion(bf16[8192,256]{1,0:T(8,128)(2,1)} %all-gather.6.cloned.1.call-done, bf16[1024,8192]{1,0:T(8,128)(2,1)} %all-gather.8.cloned.1.call-done, f32[1024]{0:T(1024)S(1)} %bitcast.61), kind=kOutput, calls=%fused_computation.6 | convolution fusion | flops 4295753728 | bytes 21499904 | tf_op jit(solution)/shard_map/dot_general | solution.py:36
  204.3 0.0 copy-done.1
  204.3 1.0 convolution_convert_fusion.2
  205.3 0.0 all-gather.12.cloned.1.call-update
  205.3 0.2 all-reduce.3.cloned.1.call-start
  205.5 0.0 copy-done
  205.6 1.9 fusion.8
  207.4 112.9 %all-gather.10.cloned.1.call-done = bf16[8192,512]{0,1:T(8,128)(2,1)} async-done(((bf16[1024,512]{0,1:T(8,128)(2,1)}), bf16[8192,512]{0,1:T(8,128)(2,1)}) %all-gather.10.cloned.1.call-update) | async-done | bytes 8388624 | tf_op jit(solution)/shard_map/all_gather | solution.py:43
  320.4 15.2 %fusion.2 = bf16[1024,512]{0,1:T(8,128)(2,1)S(1)} fusion(f32[1024,512]{0,1:T(8,128)S(1)} %bitcast.50, f32[2,1024,256]{1,2,0:T(8,128)} %fusion.8, bf16[8192,512]{0,1:T(8,128)(2,1)} %all-gather.10.cloned.1.call-done, bf16[1024,8192]{1,0:T(8,128)(2,1)} %all-gather.8.cloned.1.call-done), kind=kOutput, calls=%fused_computation.3 | convolution fusion | flops 8592031744 | bytes 30408704 | tf_op jit(solution)/shard_map/dot_general | solution.py:41
  335.6 0.0 copy-start.6
  335.6 0.0 copy-start.8
  335.7 1.2 convolution_convert_fusion.1
  336.8 0.0 copy-done.6
  336.8 1.2 convolution_convert_fusion
  338.0 0.0 all-reduce.3.cloned.1.call-update
  338.1 1.0 copy.20
  339.1 2.3 copy.21
  341.3 20.0 %all-gather.12.cloned.1.call-done = bf16[2048,256]{1,0:T(8,128)(2,1)} async-done(((bf16[256,256]{1,0:T(8,128)(2,1)}), bf16[2048,256]{1,0:T(8,128)(2,1)}) %all-gather.12.cloned.1.call-update) | async-done | bytes 1048592 | tf_op jit(solution)/shard_map/all_gather | solution.py:62
  361.4 1.4 reduce.2
  362.8 0.0 copy-start.4
  362.8 73.9 %all-reduce.3.cloned.1.call-done = (bf16[2,256,256]{2,1,0:T(8,128)(2,1)}, bf16[2,256,256]{2,1,0:T(8,128)(2,1)}) async-done(((bf16[2,256,256]{2,1,0:T(8,128)(2,1)}, bf16[2,256,256]{2,1,0:T(8,128)(2,1)}), (bf16[2,256,256]{2,1,0:T(8,128)(2,1)}, bf16[2,256,256]{2,1,0:T(8,128)(2,1)})) %all-reduce.3.cloned.1.call-update) | async-done | bytes 524304 | tf_op jit(solution)/shard_map/psum | solution.py:68
  436.7 1.4 fusion.6
  438.0 0.0 copy-start.3
  438.1 2.4 fusion.5
  (11 shorter events, 0.1 us)
Async XLA Ops:
  7.2 198.4 %copy-start = (bf16[2,256,256]{2,1,0:T(8,128)(2,1)S(1)}, bf16[2,256,256]{2,1,0:T(8,128)(2,1)}, u32[]{:S(2)}) copy-start(bf16[2,256,256]{2,1,0:T(8,128)(2,1)} %param.11) | copy-start | bytes 786436
  7.2 4.3 copy-start.10
  7.2 3.8 copy-start.5
  7.2 4.3 copy-start.9
  7.2 79.7 %all-gather.6.cloned.1.call-start = ((), (), s32[]{:S(2)}) async-start(), calls=%async_computation | async-start | bytes 4718592 | tf_op jit(solution)/shard_map/all_gather | solution.py:38
  10.2 182.5 %all-gather.8.cloned.1.call-start = ((), (), s32[]{:S(2)}) async-start(), calls=%async_computation.1 | async-start | bytes 20971520 | tf_op jit(solution)/shard_map/all_gather | solution.py:35
  10.9 309.5 %all-gather.10.cloned.1.call-start = ((), (), s32[]{:S(2)}) async-start(), calls=%async_computation.2 | async-start | bytes 9437184 | tf_op jit(solution)/shard_map/all_gather | solution.py:43
  13.5 190.8 %copy-start.1 = (bf16[1024,256]{1,0:T(8,128)(2,1)S(1)}, bf16[1024,256]{1,0:T(8,128)(2,1)}, u32[]{:S(2)}) copy-start(bf16[1024,256]{1,0:T(8,128)(2,1)} %broadcast_multiply_fusion) | copy-start | bytes 1572868
  13.5 347.9 %all-gather.12.cloned.1.call-start = ((), (), s32[]{:S(2)}) async-start(), calls=%async_computation.3 | async-start | bytes 1179648 | tf_op jit(solution)/shard_map/all_gather | solution.py:62
  205.3 231.4 %all-reduce.3.cloned.1.call-start = ((), (), s32[]{:S(2)}) async-start(), calls=%async_computation.4 | async-start | bytes 1048576 | tf_op jit(solution)/shard_map/psum | solution.py:68
  320.4 15.3 %copy-start.2 = (bf16[1024,512]{0,1:T(8,128)(2,1)S(1)}, bf16[1024,512]{0,1:T(8,128)(2,1)}, u32[]{:S(2)}) copy-start(bf16[1024,512]{0,1:T(8,128)(2,1)} %convert_multiply_fusion) | copy-start | bytes 3145732
  335.6 1.2 copy-start.6
  335.6 27.1 %copy-start.8 = (f32[1,256,256]{2,1,0:T(8,128)S(1)}, f32[1,256,256]{2,1,0:T(8,128)}, u32[]{:S(2)}) copy-start(f32[1,256,256]{2,1,0:T(8,128)} %param.12) | copy-start | bytes 786436
  336.8 101.2 %copy-start.7 = (f32[2,256,256]{2,1,0:T(8,128)S(1)}, f32[2,256,256]{2,1,0:T(8,128)}, u32[]{:S(2)}) copy-start(f32[2,256,256]{2,1,0:T(8,128)} %param.13) | copy-start | bytes 1572868
  362.8 77.7 %copy-start.4 = (f32[1,256,256]{2,1,0:T(8,128)}, f32[1,256,256]{2,1,0:T(8,128)S(1)}, u32[]{:S(2)}) copy-start(f32[1,256,256]{2,1,0:T(8,128)S(1)} %convert_subtract_fusion) | copy-start | bytes 786436
  438.0 2.4 copy-start.3
Sparse Core Ops, SparseCore 0:
  10.7 76.0 all-gather.5
  88.4 104.1 all-gather.7
  195.4 124.9 all-gather.9
  322.9 38.4 all-gather.11
  365.3 71.3 all-reduce.2
